TPU v7x, 32 devices: a whole 2x2x4 slice. The times are simulated.
32 devices in a mesh: groups: 2 (over y), dp: 4 (over z), tensor: 4 (over x, core).
Axes of the slice: x: 2, y: 2, z: 4, core: 2. Of those that a mesh axis runs over, the one named last changes fastest.
Arguments:
- tokens: bfloat16 [1024, 16384], P(('groups', 'dp')), parts along dimension 0, may hold values from -6 to 6
- gate_weight: bfloat16 [16384, 512], P('dp', 'tensor'), may hold values from -0.046875 to 0.046875
- up_weight: bfloat16 [16384, 512], P('dp', 'tensor'), may hold values from -0.046875 to 0.046875
- down_weight: bfloat16 [512, 16384], P('tensor', 'dp'), may hold values from -0.5 to 0.5
- gate_mask: int32 [128, 4], P(None, 'tensor'), may hold values from 0 to 1, as said below
- up_mask: int32 [128, 4], P(None, 'tensor'), may hold values from 0 to 1, as said below
- down_mask: int32 [4, 128], P('tensor'), may hold values from 0 to 1, as said below
Outputs:
- mixed: bfloat16 [1024, 16384], P(('groups', 'dp'), 'tensor'), parts along dimension 0
There are 2 independent parts, one for each index of `groups`. A program takes and returns all parts, laid end to end along the dimension named above; an argument that names none is the same for every part. Nothing has to cross between parts.
Inputs may be any that keep to these rules, and one draw needn't show every extreme that they name: `gate_mask`: each block flag; every shard of a mask that one device holds for the layer's weights (32 blocks: rows of one dp index and hidden units of one tensor index) keeps between 8 and 24 blocks, and some such shard keeps exactly 24 in every draw. `up_mask`: as for gate_mask, drawn apart. `down_mask`: as for gate_mask, for the down projection's shards (1 hidden blocks of one tensor index times 32 width blocks of one dp index).
All inputs are finite; a program needn't handle non-finite values.
Results may differ from a plain program's by a relative error of at most 0.006.
Values may be sent and summed in bfloat16 or wider, within the bound.
A program may use at most 64 MiB of HBM per device.

v0:
```python
import jax
import jax.numpy as jnp
from jax import lax
from jax.sharding import PartitionSpec as P

BS = 128


def expand_mask(mask):
    return jnp.repeat(jnp.repeat(mask, BS, axis=0), BS, axis=1).astype(jnp.bfloat16)


def shards(tokens, gate_weight, up_weight, down_weight, gate_mask, up_mask, down_mask):
    dp_index = lax.axis_index("dp")
    row_blocks = gate_weight.shape[0] // BS
    row_start = dp_index * row_blocks
    gate_pruned = gate_weight * expand_mask(
        lax.dynamic_slice_in_dim(gate_mask, row_start, row_blocks, 0)
    )
    up_pruned = up_weight * expand_mask(lax.dynamic_slice_in_dim(up_mask, row_start, row_blocks, 0))
    gate_part = jnp.dot(
        tokens,
        lax.all_gather(gate_pruned, "dp", axis=0, tiled=True),
        preferred_element_type=jnp.float32,
    )
    up_part = jnp.dot(
        tokens,
        lax.all_gather(up_pruned, "dp", axis=0, tiled=True),
        preferred_element_type=jnp.float32,
    )
    hidden = (jax.nn.silu(gate_part) * up_part).astype(jnp.bfloat16)
    down_pruned = down_weight * expand_mask(
        lax.dynamic_slice_in_dim(down_mask, row_start, row_blocks, 1)
    )
    partial_out = jnp.dot(
        hidden,
        lax.all_gather(down_pruned, "dp", axis=1, tiled=True),
        preferred_element_type=jnp.float32,
    )
    rounded = partial_out.astype(jnp.bfloat16).astype(jnp.float32)
    return lax.psum_scatter(rounded.astype(jnp.bfloat16), "tensor", scatter_dimension=1, tiled=True)


def solution(mesh):
    placed = (
        P(("groups", "dp"), None),
        P("dp", "tensor"),
        P("dp", "tensor"),
        P("tensor", "dp"),
        P(None, "tensor"),
        P(None, "tensor"),
        P("tensor", None),
    )
    return jax.shard_map(
        shards, mesh=mesh, in_specs=placed, out_specs=P(("groups", "dp"), "tensor"), check_vma=False
    )
```

profile of v0, /device:TPU:3, one launch (start us, length us, event | category | flops | bytes accessed | tf_op | source)
XLA Modules:
  0.0 314.0 jit_solution(14790526022675821337)
XLA Ops:
  6.5 0.0 copy-start.1
  6.5 0.0 copy-start
  6.5 0.0 all-gather.4.cloned.1.call-start
  6.5 0.8 fusion.9
  7.4 0.1 broadcast_bitcast_fusion.2
  7.4 2.5 broadcast_multiply_fusion.2
  10.0 0.0 all-gather.4.cloned.1.call-update
  10.0 0.0 all-gather.6.cloned.1.call-start
  10.1 0.1 broadcast_bitcast_fusion.1
  10.1 2.6 broadcast_multiply_fusion.1
  12.7 0.0 all-gather.6.cloned.1.call-update
  12.7 0.0 all-gather.8.cloned.1.call-start
  12.8 0.0 copy-done.1
  12.8 0.1 fusion.13
  12.9 0.1 broadcast_bitcast_fusion
  12.9 0.0 copy-done
  12.9 1.1 broadcast_multiply_fusion
  14.0 0.0 all-gather.8.cloned.1.call-update
  14.0 0.0 reduce-scatter.2.cloned.1.call-start
  14.1 78.1 %all-gather.4.cloned.1.call-done = bf16[16384,128]{1,0:T(8,128)(2,1)} async-done(((bf16[4096,128]{1,0:T(8,128)(2,1)}), bf16[16384,128]{1,0:T(8,128)(2,1)}) %all-gather.4.cloned.1.call-update) | async-done | bytes 4194320 | tf_op jit(solution)/shard_map/all_gather | solution.py:23
  92.2 4.7 %convolution_bitcast_fusion.1 = f32[128,128]{0,1:T(8,128)S(1)} fusion(bf16[16384,128]{1,0:T(8,128)(2,1)} %all-gather.4.cloned.1.call-done, bf16[128,16384]{1,0:T(8,128)(2,1)} %param.7), kind=kOutput, calls=%fused_computation.3 | convolution fusion | flops 536870912 | bytes 8454144 | tf_op jit(solution)/shard_map/dot_general | solution.py:21
  96.9 76.1 %all-gather.6.cloned.1.call-done = bf16[16384,128]{1,0:T(8,128)(2,1)} async-done(((bf16[4096,128]{1,0:T(8,128)(2,1)}), bf16[16384,128]{1,0:T(8,128)(2,1)}) %all-gather.6.cloned.1.call-update) | async-done | bytes 4194320 | tf_op jit(solution)/shard_map/all_gather | solution.py:28
  173.1 80.9 %all-gather.8.cloned.1.call-done = bf16[128,16384]{1,0:T(8,128)(2,1)} async-done(((bf16[128,4096]{1,0:T(8,128)(2,1)}), bf16[128,16384]{1,0:T(8,128)(2,1)}) %all-gather.8.cloned.1.call-update) | async-done | bytes 4194320 | tf_op jit(solution)/shard_map/all_gather | solution.py:37
  254.0 11.3 %convolution_convert_fusion = bf16[128,16384]{1,0:T(8,128)(2,1)} fusion(bf16[128,16384]{1,0:T(8,128)(2,1)} %all-gather.8.cloned.1.call-done, bf16[16384,128]{1,0:T(8,128)(2,1)} %all-gather.6.cloned.1.call-done, bf16[128,16384]{1,0:T(8,128)(2,1)} %param.7, f32[128,128]{0,1:T(8,128)S(1)} %convolution_bitcast_fusion.1), kind=kOutput, calls=%fused_computation | convolution fusion | flops 1075937280 | bytes 16842752 | tf_op jit(solution)/shard_map/dot_general | solution.py:35
  265.2 0.0 reduce-scatter.2.cloned.1.call-update
  265.3 42.2 %reduce-scatter.2.cloned.1.call-done = bf16[128,4096]{1,0:T(8,128)(2,1)} async-done(((bf16[128,16384]{1,0:T(8,128)(2,1)}), bf16[128,4096]{1,0:T(8,128)(2,1)}) %reduce-scatter.2.cloned.1.call-update) | async-done | bytes 1048592 | tf_op jit(solution)/shard_map/reduce_scatter | solution.py:41
Async XLA Ops:
  6.5 6.2 %copy-start.1 = (s32[1,128]{1,0:T(1,128)S(1)}, s32[1,128]{1,0:T(1,128)}, u32[]{:S(2)}) copy-start(s32[1,128]{1,0:T(1,128)} %param.13) | copy-start | bytes 1540
  6.5 6.4 %copy-start = (bf16[128,4096]{1,0:T(8,128)(2,1)S(1)}, bf16[128,4096]{1,0:T(8,128)(2,1)}, u32[]{:S(2)}) copy-start(bf16[128,4096]{1,0:T(8,128)(2,1)} %param.10) | copy-start | bytes 3145732
  6.5 85.6 %all-gather.4.cloned.1.call-start = ((), (), s32[]{:S(2)}) async-start(), calls=%async_computation.1 | async-start | bytes 5242880 | tf_op jit(solution)/shard_map/all_gather | solution.py:23
  10.0 163.1 %all-gather.6.cloned.1.call-start = ((), (), s32[]{:S(2)}) async-start(), calls=%async_computation.2 | async-start | bytes 5242880 | tf_op jit(solution)/shard_map/all_gather | solution.py:28
  12.7 241.2 %all-gather.8.cloned.1.call-start = ((), (), s32[]{:S(2)}) async-start(), calls=%async_computation.3 | async-start | bytes 5242880 | tf_op jit(solution)/shard_map/all_gather | solution.py:37
  14.0 293.5 %reduce-scatter.2.cloned.1.call-start = ((), (), s32[]{:S(2)}) async-start(), calls=%async_computation.4 | async-start | bytes 5242880 | tf_op jit(solution)/shard_map/reduce_scatter | solution.py:41
Sparse Core Ops, SparseCore 0:
  10.1 81.9 all-gather.3
  93.7 79.2 all-gather.5
  174.6 79.2 all-gather.7
  265.4 42.0 reduce-scatter.1
where the time goes:
time: 317 us; the launch traced here: 314 us
  waiting for transfers between devices  277 us (87%)
  matrix products  16 us (5%)
  between operations  13.1 us (4%)
  other arithmetic  7.06 us (2%)
    all_gather x1, waiting for transfers between devices, shards(): lax.all_gather(down_pruned, 'dp', axis=1, tiled=True)  80.9 us
    all_gather x1, waiting for transfers between devices, shards(): lax.all_gather(gate_pruned, 'dp', axis=0, tiled=True)  78.1 us
    all_gather x1, waiting for transfers between devices, shards(): lax.all_gather(up_pruned, 'dp', axis=0, tiled=True)  76.1 us
    reduce_scatter x1, waiting for transfers between devices, shards(): lax.psum_scatter(rounded.astype(jnp.bfloat16), 'tensor', scatter_dimensio...  42.2 us
    dot_general x1, matrix products, shards(): jnp.dot(hidden, lax.all_gather(down_pruned, 'dp', axis=1, tiled=True), pr...  11.3 us
  transfers between devices with their start and end apart: 4, of which 4 were waited for; matrix products, arithmetic and copies ran while one was open for 3% of the time, Pallas kernels for 0%

commit v1 on v0

--- a/solution.py
+++ b/solution.py
@@ -1,16 +1,22 @@
+import functools
+
 import jax
 import jax.numpy as jnp
 from jax import lax
+from jax.experimental import pallas as pl
+from jax.experimental.pallas import tpu as pltpu
 from jax.sharding import PartitionSpec as P
 
 BS = 128
+MESH = pl.DeviceIdType.MESH
+CHUNKS = 4
 
 
 def expand_mask(mask):
     return jnp.repeat(jnp.repeat(mask, BS, axis=0), BS, axis=1).astype(jnp.bfloat16)
 
 
-def shards(tokens, gate_weight, up_weight, down_weight, gate_mask, up_mask, down_mask):
+def gathered(tokens, gate_weight, up_weight, down_weight, gate_mask, up_mask, down_mask):
     dp_index = lax.axis_index("dp")
     row_blocks = gate_weight.shape[0] // BS
     row_start = dp_index * row_blocks
@@ -37,11 +43,267 @@
         lax.all_gather(down_pruned, "dp", axis=1, tiled=True),
         preferred_element_type=jnp.float32,
     )
-    rounded = partial_out.astype(jnp.bfloat16).astype(jnp.float32)
-    return lax.psum_scatter(rounded.astype(jnp.bfloat16), "tensor", scatter_dimension=1, tiled=True)
+    return lax.psum_scatter(
+        partial_out.astype(jnp.bfloat16), "tensor", scatter_dimension=1, tiled=True
+    )
+
+
+def kernel(n, tok_hbm, gate_hbm, up_hbm, down_hbm, gmask, umask, dmask, out,
+           T, W, PC, G, psend, precv, H,
+           ch_s, ch_r, ip_s, ip_r, y_s, y_r, tz_s, tz_r, tx_s, tx_r, tc_s, tc_r,
+           p_s, p_r, h_s, h_r, ld):
+    g = lax.axis_index("groups")
+    z = lax.axis_index("dp")
+    t = lax.axis_index("tensor")
+    rows = tok_hbm.shape[0]
+    width = gate_hbm.shape[0]
+    hid = gate_hbm.shape[1]
+    half = hid // 2
+    quarter = rows // n
+    cw = width // CHUNKS
+    blocks = width // BS
+    zero = jnp.int32(0)
+    t_core = jnp.where(lax.rem(t, 2) == zero, t + 1, t - 1)
+    t_x = lax.rem(t + 2, n)
+
+    def mod(a):
+        return lax.rem(a + 2 * n, n)
+
+    def remote(src, dst, ss, rs, **where):
+        return pltpu.make_async_remote_copy(
+            src_ref=src, dst_ref=dst, send_sem=ss, recv_sem=rs, device_id=where,
+            device_id_type=MESH)
+
+    own_cols = pl.ds(pl.multiple_of(z * width, 128), width)
+    load_down = pltpu.make_async_copy(
+        down_hbm.at[pl.ds(pl.multiple_of(g * half, half), half), :], PC.at[z], ld.at[0])
+    load_tok = pltpu.make_async_copy(
+        tok_hbm.at[:, own_cols], T.at[pl.ds(pl.multiple_of(z * rows, rows), rows), :], ld.at[1])
+    load_gate = pltpu.make_async_copy(gate_hbm, W.at[:, pl.ds(0, hid)], ld.at[2])
+    load_up = pltpu.make_async_copy(up_hbm, W.at[:, pl.ds(hid, hid)], ld.at[3])
+    load_down.start()
+
+    barrier = pltpu.get_barrier_semaphore()
+    for d in range(1, n):
+        pl.semaphore_signal(barrier, inc=1, device_id={"dp": mod(z + d)}, device_id_type=MESH)
+        pl.semaphore_signal(barrier, inc=1, device_id={"tensor": mod(t + d)}, device_id_type=MESH)
+    pl.semaphore_signal(barrier, inc=1, device_id={"groups": 1 - g}, device_id_type=MESH)
+    load_gate.start()
+    load_up.start()
+    load_tok.start()
+
+    load_down.wait()
+    for b in range(blocks):
+        keep = dmask[z * blocks + b].astype(jnp.float32)
+        cols = pl.ds(b * BS, BS)
+        PC[z, :, cols] = (PC[z, :, cols].astype(jnp.float32) * keep).astype(jnp.bfloat16)
+    pl.semaphore_wait(barrier, 2 * (n - 1) + 1)
+
+    pending = []
+
+    def go(copy, cond=None):
+        pending.append((copy, cond))
+        if cond is None:
+            copy.start()
+        else:
+            pl.when(cond)(copy.start)
+
+    def chunk(c):
+        return pl.ds(c * cw, cw)
+
+    def g_rows(ts, h):
+        return pl.ds(pl.multiple_of(ts * hid + h * half, half), half)
+
+    def chain(direction, r, c):
+        k = z - r if direction == 0 else z + r
+        to = z + 1 if direction == 0 else z - 1
+        ok = (k >= 0) & (to < n) if direction == 0 else (k < n) & (to >= 0)
+        kk = mod(k)
+        return remote(
+            PC.at[kk, :, chunk(c)], PC.at[kk, :, chunk(c)], ch_s.at[direction, r, c],
+            ch_r.at[direction, r, c], dp=mod(to)), ok
+
+    def dispatch(k, slot, c, ok):
+        copy = remote(
+            PC.at[k, :, chunk(c)], G.at[g_rows(t, g), chunk(c)], ip_s.at[slot, c],
+            ip_r.at[t, c], tensor=k)
+        go(copy, ok & (k != t))
+
+    def across(e, c):
+        ts = mod(t + e)
+        ref = G.at[g_rows(ts, g), chunk(c)]
+        return remote(ref, ref, y_s.at[e, c], y_r.at[e, c], groups=1 - g)
+
+    def arrived(e, c):
+        ts = mod(t + e)
+        ref = G.at[g_rows(ts, g), chunk(c)]
+        return remote(ref, ref, ip_s.at[0, c], ip_r.at[ts, c], tensor=ts)
+
+    crossings = [[across(e, c) for e in range(n)] for c in range(CHUNKS)]
+
+    def owner_round(r):
+        @pl.when(jnp.abs(z - t) == r)
+        def _():
+            for c in range(CHUNKS):
+                G[g_rows(t, g), chunk(c)] = PC[t, :, chunk(c)]
+                crossings[c][0].start()
+                for e in range(1, n):
+                    arrived(e, c).wait_recv()
+                    crossings[c][e].start()
+
+    for c in range(CHUNKS):
+        for direction in range(2):
+            copy, ok = chain(direction, 0, c)
+            go(copy, ok)
+    for c in range(CHUNKS):
+        dispatch(z, 0, c, True)
+
+    def token_piece(s, q):
+        return T.at[pl.ds(pl.multiple_of(s * rows + q * quarter, quarter), quarter), :]
+
+    for d in (2, 1, 3):
+        k = mod(z + d)
+        go(remote(
+            tok_hbm.at[pl.ds(pl.multiple_of(t * quarter, quarter), quarter),
+                       pl.ds(pl.multiple_of(k * width, 128), width)],
+            token_piece(z, t), tz_s.at[d - 1], tz_r.at[d - 1], dp=k))
+
+    def relay_tokens(d):
+        s = mod(z - d)
+        mine = token_piece(s, t)
+        remote(mine, mine, tz_s.at[d - 1], tz_r.at[d - 1], dp=s).wait_recv()
+        go(remote(mine, mine, tx_s.at[d - 1], tx_r.at[d - 1], tensor=t_x))
+        go(remote(mine, mine, tc_s.at[0, d - 1], tc_r.at[0, d - 1], tensor=t_core))
+
+    def relay_x(d):
+        s = mod(z - d)
+        other = token_piece(s, t_x)
+        remote(other, other, tx_s.at[d - 1], tx_r.at[d - 1], tensor=t_x).wait_recv()
+        go(remote(other, other, tc_s.at[1, d - 1], tc_r.at[1, d - 1], tensor=t_core))
+
+    def products(s):
+        return jnp.dot(
+            T[pl.ds(pl.multiple_of(s * rows, rows), rows), :], W[...],
+            preferred_element_type=jnp.float32)
+
+    def finish_tokens(d):
+        s = mod(z - d)
+        for hop, q in enumerate((t_core, lax.rem(t_core + 2, n))):
+            piece = token_piece(s, q)
+            remote(piece, piece, tc_s.at[hop, d - 1], tc_r.at[hop, d - 1],
+                   tensor=t_core).wait_recv()
+        psend[d - 1] = products(s).astype(jnp.bfloat16)
+        go(remote(psend.at[d - 1], precv.at[d - 1], p_s.at[d - 1], p_r.at[d - 1], dp=s))
+
+    load_gate.wait()
+    load_up.wait()
+
+    @pl.loop(0, blocks)
+    def _(b):
+        at = pl.ds(pl.multiple_of(b * BS, BS), BS)
+        gk = gmask[z * blocks + b].astype(jnp.float32)
+        uk = umask[z * blocks + b].astype(jnp.float32)
+        W[at, pl.ds(0, hid)] = (W[at, pl.ds(0, hid)].astype(jnp.float32) * gk).astype(jnp.bfloat16)
+        W[at, pl.ds(hid, hid)] = (W[at, pl.ds(hid, hid)].astype(jnp.float32) * uk).astype(jnp.bfloat16)
+
+    load_tok.wait()
+    own = products(z)
+    owner_round(0)
+
+    for r in range(1, n):
+        for c in range(CHUNKS):
+            for direction in range(2):
+                k = z - r if direction == 0 else z + r
+                ok = k >= 0 if direction == 0 else k < n
+                kk = mod(k)
+                piece = PC.at[kk, :, chunk(c)]
+                came = remote(piece, piece, ch_s.at[direction, r - 1, c],
+                              ch_r.at[direction, r - 1, c], dp=mod(z + 1))
+                pl.when(ok)(came.wait_recv)
+                if r < n - 1:
+                    copy, also = chain(direction, r, c)
+                    go(copy, ok & also)
+                dispatch(kk, 2 * r - 1 + direction, c, ok)
+        owner_round(r)
+        relay_tokens((1, 3, 2)[r - 1])
+    for d in (1, 3, 2):
+        relay_x(d)
+    for d in (1, 3, 2):
+        finish_tokens(d)
+
+    total = own
+    for d in range(1, n):
+        ref = precv.at[d - 1]
+        remote(ref, ref, p_s.at[d - 1], p_r.at[d - 1], dp=mod(z + d)).wait_recv()
+        total = total + precv[d - 1].astype(jnp.float32)
+    gate, up = total[:, :hid], total[:, hid:]
+    mine = pl.ds(pl.multiple_of(t * hid, hid), hid)
+    H[:, mine] = (gate / (1.0 + jnp.exp(-gate)) * up).astype(jnp.bfloat16)
+    for d in range(1, n):
+        go(remote(H.at[:, mine], H.at[:, mine], h_s.at[d - 1], h_r.at[d - 1], tensor=mod(t + d)))
+    for d in range(1, n):
+        theirs = H.at[:, pl.ds(pl.multiple_of(mod(t - d) * hid, hid), hid)]
+        remote(theirs, theirs, h_s.at[d - 1], h_r.at[d - 1], tensor=mod(t + d)).wait_recv()
+
+    for c in range(CHUNKS):
+        for e in range(n):
+            ts = mod(t + e)
+            ref = G.at[g_rows(ts, 1 - g), chunk(c)]
+            remote(ref, ref, y_s.at[e, c], y_r.at[e, c], groups=1 - g).wait_recv()
+        out[:, chunk(c)] = jnp.dot(
+            H[...], G[:, chunk(c)], preferred_element_type=jnp.float32).astype(jnp.bfloat16)
+
+    for copy, cond in pending:
+        if cond is None:
+            copy.wait_send()
+        else:
+            pl.when(cond)(copy.wait_send)
+    for row in crossings:
+        for copy in row:
+            copy.wait_send()
+
+
+def fused(n, tokens, gate_weight, up_weight, down_weight, gate_mask, up_mask, down_mask):
+    rows = tokens.shape[0]
+    width, hid = gate_weight.shape
+    bf16 = jnp.bfloat16
+    dma = pltpu.SemaphoreType.DMA
+    anyspec = pl.BlockSpec(memory_space=pl.ANY)
+    smem = pl.BlockSpec(memory_space=pltpu.SMEM)
+    return pl.pallas_call(
+        functools.partial(kernel, n),
+        out_shape=jax.ShapeDtypeStruct((rows, width), bf16),
+        in_specs=[anyspec] * 4 + [smem] * 3,
+        out_specs=pl.BlockSpec(memory_space=pltpu.VMEM),
+        scratch_shapes=[
+            pltpu.VMEM((n * rows, width), bf16),
+            pltpu.VMEM((width, 2 * hid), bf16),
+            pltpu.VMEM((n, hid // 2, width), bf16),
+            pltpu.VMEM((n * hid, width), bf16),
+            pltpu.VMEM((n - 1, rows, 2 * hid), bf16),
+            pltpu.VMEM((n - 1, rows, 2 * hid), bf16),
+            pltpu.VMEM((rows, n * hid), bf16),
+            dma((2, n - 1, CHUNKS)), dma((2, n - 1, CHUNKS)),
+            dma((2 * n - 1, CHUNKS)), dma((n, CHUNKS)),
+            dma((n, CHUNKS)), dma((n, CHUNKS)),
+            dma((n - 1,)), dma((n - 1,)),
+            dma((n - 1,)), dma((n - 1,)),
+            dma((2, n - 1)), dma((2, n - 1)),
+            dma((n - 1,)), dma((n - 1,)),
+            dma((n - 1,)), dma((n - 1,)),
+            dma((4,)),
+        ],
+        compiler_params=pltpu.CompilerParams(
+            collective_id=0, has_side_effects=True, vmem_limit_bytes=40 * 1024 * 1024),
+        cost_estimate=pl.CostEstimate(
+            flops=2 * rows * n * width * 3 * hid, bytes_accessed=16 * 1024 * 1024,
+            transcendentals=rows * hid),
+    )(tokens, gate_weight, up_weight, down_weight, gate_mask.reshape(-1), up_mask.reshape(-1),
+      down_mask.reshape(-1))
 
 
 def solution(mesh):
+    n_dp, n_tensor, n_groups = mesh.shape["dp"], mesh.shape["tensor"], mesh.shape["groups"]
     placed = (
         P(("groups", "dp"), None),
         P("dp", "tensor"),
@@ -51,6 +313,9 @@
         P(None, "tensor"),
         P("tensor", None),
     )
+    body = gathered
+    if n_dp == 4 and n_tensor == 4 and n_groups == 2:
+        body = functools.partial(fused, n_dp)
     return jax.shard_map(
-        shards, mesh=mesh, in_specs=placed, out_specs=P(("groups", "dp"), "tensor"), check_vma=False
-    )
+        body, mesh=mesh, in_specs=placed, out_specs=P(("groups", "dp"), "tensor"), check_vma=False
+    )

time: 317 us -> 105 us (0.33)
  waiting for transfers between devices: 277 us -> 0 us
  Pallas kernels: 0 us -> 95.5 us
  matrix products: 16 us -> 0 us
  between operations: 13.1 us -> 0.02 us
  local copies, waits for them, and re-layouts: 0.22 us -> 8.8 us
  other arithmetic: 7.06 us -> 0 us
    all_gather x3 -> x0, waiting for transfers between devices: 235 us -> none  [the longest x1 80.9 us: shards(): lax.all_gather(down_pruned, 'dp', axis=1, tiled=True)]
    pallas_call x0 -> x1, Pallas kernels: none -> 95.5 us  [fused(): pl.pallas_call(functools.partial(kernel, n), out_shape=jax.ShapeDtypeStru...]
    reduce_scatter x1 -> x0, waiting for transfers between devices: 42.2 us -> none  [shards(): lax.psum_scatter(rounded.astype(jnp.bfloat16), 'tensor', scatter_dimensio...]
    dot_general x2 -> x0, matrix products: 16 us -> none  [the longest x1 11.3 us: shards(): jnp.dot(hidden, lax.all_gather(down_pruned, 'dp', axis=1, tiled=True), pr...]
    unnamed x4 -> x15, local copies, waits for them, and re-layouts: 0.01 us -> 8.8 us
    mul x3 -> x0, other arithmetic: 6.14 us -> none  [the longest x1 2.57 us: shards(): up_weight * expand_mask(lax.dynamic_slice_in_dim(up_mask, row_start, row_...]
  transfers between devices with their start and end apart: 4 -> 0, of which waited for: 4 -> 0; matrix products, arithmetic and copies ran while one was open for 3% -> 0% of each run, Pallas kernels for 0% -> 0%
where the time goes in v1:
time: 105 us; the launch traced here: 104 us
  Pallas kernels  95.5 us (91%)
  local copies, waits for them, and re-layouts  8.8 us (8%)
    pallas_call x1, Pallas kernels, fused(): pl.pallas_call(functools.partial(kernel, n), out_shape=jax.ShapeDtypeStru...  95.5 us
    unnamed x15, local copies, waits for them, and re-layouts  8.8 us

profile of v1, /device:TPU:3, one launch (start us, length us, event | category | flops | bytes accessed | tf_op | source)
XLA Modules:
  0.0 104.4 jit_solution(2395160127618231014)
XLA Ops:
  0.0 0.0 copy-start
  0.0 2.2 %copy-done = bf16[128,16384]{1,0:T(8,128)(2,1)S(1)} copy-done((bf16[128,16384]{1,0:T(8,128)(2,1)S(1)}, bf16[128,16384]{1,0:T(8,128)(2,1)}, u32[]{:S(2)}) %copy-start) | copy-done | bytes 4194328
  2.2 0.0 copy-start.1
  2.2 1.2 %copy-done.1 = bf16[4096,128]{1,0:T(8,128)(2,1)S(1)} copy-done((bf16[4096,128]{1,0:T(8,128)(2,1)S(1)}, bf16[4096,128]{1,0:T(8,128)(2,1)}, u32[]{:S(2)}) %copy-start.1) | copy-done | bytes 1048600
  3.4 0.0 copy-start.2
  3.4 1.2 %copy-done.2 = bf16[4096,128]{1,0:T(8,128)(2,1)S(1)} copy-done((bf16[4096,128]{1,0:T(8,128)(2,1)S(1)}, bf16[4096,128]{1,0:T(8,128)(2,1)}, u32[]{:S(2)}) %copy-start.2) | copy-done | bytes 1048600
  4.6 0.0 copy-start.3
  4.6 1.2 %copy-done.3 = bf16[128,4096]{1,0:T(8,128)(2,1)S(1)} copy-done((bf16[128,4096]{1,0:T(8,128)(2,1)S(1)}, bf16[128,4096]{1,0:T(8,128)(2,1)}, u32[]{:S(2)}) %copy-start.3) | copy-done | bytes 1048600
  5.9 0.0 copy-start.4
  5.9 0.7 copy-done.4
  6.5 0.0 copy-start.5
  6.5 0.7 copy-done.5
  7.2 0.0 copy-start.6
  7.2 0.7 copy-done.6
  7.8 95.5 %shard_map.73 = bf16[128,4096]{1,0:T(8,128)(2,1)S(1)} custom-call(bf16[128,16384]{1,0:T(8,128)(2,1)S(1)} %copy-done, bf16[4096,128]{1,0:T(8,128)(2,1)S(1)} %copy-done.1, bf16[4096,128]{1,0:T(8,128)(2,1)S(1)} %copy-done.2, bf16[128,4096]{1,0:T(8,128)(2,1)S(1)} %copy-done.3, s32[128]{0:T(128)S(1)} %bitcast.3, s32[128]{0:T(128)S(1)} %bitcast.4, s32[128]{0:T(128)S(1)} %bitcast.5), custom_call_target="tpu_custom_call" | custom-call | flops 1610612736 | bytes 16777216 | tf_op jit(solution)/shard_map/pallas_call | solution.py:273
  103.4 1.0 copy.9
Async XLA Ops:
  0.0 2.2 %copy-start = (bf16[128,16384]{1,0:T(8,128)(2,1)S(1)}, bf16[128,16384]{1,0:T(8,128)(2,1)}, u32[]{:S(2)}) copy-start(bf16[128,16384]{1,0:T(8,128)(2,1)} %tok_hbm.1) | copy-start | bytes 12582916
  2.2 1.2 %copy-start.1 = (bf16[4096,128]{1,0:T(8,128)(2,1)S(1)}, bf16[4096,128]{1,0:T(8,128)(2,1)}, u32[]{:S(2)}) copy-start(bf16[4096,128]{1,0:T(8,128)(2,1)} %gate_hbm.1) | copy-start | bytes 3145732
  3.4 1.2 %copy-start.2 = (bf16[4096,128]{1,0:T(8,128)(2,1)S(1)}, bf16[4096,128]{1,0:T(8,128)(2,1)}, u32[]{:S(2)}) copy-start(bf16[4096,128]{1,0:T(8,128)(2,1)} %up_hbm.1) | copy-start | bytes 3145732
  4.6 1.2 %copy-start.3 = (bf16[128,4096]{1,0:T(8,128)(2,1)S(1)}, bf16[128,4096]{1,0:T(8,128)(2,1)}, u32[]{:S(2)}) copy-start(bf16[128,4096]{1,0:T(8,128)(2,1)} %down_hbm.1) | copy-start | bytes 3145732
  5.9 0.7 copy-start.4
  6.5 0.7 copy-start.5
  7.2 0.7 copy-start.6

commit v2 on v1

--- a/solution.py
+++ b/solution.py
@@ -48,8 +48,8 @@
     )
 
 
-def kernel(n, tok_hbm, gate_hbm, up_hbm, down_hbm, gmask, umask, dmask, out,
-           T, W, PC, G, psend, precv, H,
+def kernel(n, tok_hbm, gate_hbm, up_hbm, down_hbm, gmask_hbm, umask_hbm, dmask_hbm, out,
+           gmask, umask, dmask, T, W, PC, G, psend, precv, H,
            ch_s, ch_r, ip_s, ip_r, y_s, y_r, tz_s, tz_r, tx_s, tx_r, tc_s, tc_r,
            p_s, p_r, h_s, h_r, ld):
     g = lax.axis_index("groups")
@@ -81,6 +81,11 @@
         tok_hbm.at[:, own_cols], T.at[pl.ds(pl.multiple_of(z * rows, rows), rows), :], ld.at[1])
     load_gate = pltpu.make_async_copy(gate_hbm, W.at[:, pl.ds(0, hid)], ld.at[2])
     load_up = pltpu.make_async_copy(up_hbm, W.at[:, pl.ds(hid, hid)], ld.at[3])
+    load_masks = [
+        pltpu.make_async_copy(src, dst, ld.at[4 + m])
+        for m, (src, dst) in enumerate(
+            ((dmask_hbm, dmask), (gmask_hbm, gmask), (umask_hbm, umask)))]
+    load_masks[0].start()
     load_down.start()
 
     barrier = pltpu.get_barrier_semaphore()
@@ -88,10 +93,13 @@
         pl.semaphore_signal(barrier, inc=1, device_id={"dp": mod(z + d)}, device_id_type=MESH)
         pl.semaphore_signal(barrier, inc=1, device_id={"tensor": mod(t + d)}, device_id_type=MESH)
     pl.semaphore_signal(barrier, inc=1, device_id={"groups": 1 - g}, device_id_type=MESH)
+    load_masks[1].start()
+    load_masks[2].start()
     load_gate.start()
     load_up.start()
     load_tok.start()
 
+    load_masks[0].wait()
     load_down.wait()
     for b in range(blocks):
         keep = dmask[z * blocks + b].astype(jnp.float32)
@@ -195,6 +203,8 @@
         psend[d - 1] = products(s).astype(jnp.bfloat16)
         go(remote(psend.at[d - 1], precv.at[d - 1], p_s.at[d - 1], p_r.at[d - 1], dp=s))
 
+    load_masks[1].wait()
+    load_masks[2].wait()
     load_gate.wait()
     load_up.wait()
 
@@ -268,14 +278,15 @@
     width, hid = gate_weight.shape
     bf16 = jnp.bfloat16
     dma = pltpu.SemaphoreType.DMA
-    anyspec = pl.BlockSpec(memory_space=pl.ANY)
-    smem = pl.BlockSpec(memory_space=pltpu.SMEM)
+    hbm = pl.BlockSpec(memory_space=pltpu.HBM)
+    flags = pltpu.SMEM(gate_mask.shape[:1], jnp.int32)
     return pl.pallas_call(
         functools.partial(kernel, n),
         out_shape=jax.ShapeDtypeStruct((rows, width), bf16),
-        in_specs=[anyspec] * 4 + [smem] * 3,
+        in_specs=[hbm] * 7,
         out_specs=pl.BlockSpec(memory_space=pltpu.VMEM),
         scratch_shapes=[
+            flags, flags, flags,
             pltpu.VMEM((n * rows, width), bf16),
             pltpu.VMEM((width, 2 * hid), bf16),
             pltpu.VMEM((n, hid // 2, width), bf16),
@@ -291,7 +302,7 @@
             dma((2, n - 1)), dma((2, n - 1)),
             dma((n - 1,)), dma((n - 1,)),
             dma((n - 1,)), dma((n - 1,)),
-            dma((4,)),
+            dma((7,)),
         ],
         compiler_params=pltpu.CompilerParams(
             collective_id=0, has_side_effects=True, vmem_limit_bytes=40 * 1024 * 1024),

time: 105 us -> 104 us (level)
  no operation moved by 1% of the time
where the time goes in v2:
time: 104 us
  Pallas kernels  95 us (91%)
  local copies, waits for them, and re-layouts  8.8 us (8%)
    pallas_call x1, Pallas kernels, fused(): pl.pallas_call(functools.partial(kernel, n), out_shape=jax.ShapeDtypeStru...  95 us
    unnamed x15, local copies, waits for them, and re-layouts  8.8 us

profile of v2, /device:TPU:3, one launch (start us, length us, event | category | flops | bytes accessed | tf_op | source)
XLA Modules:
  0.0 103.8 jit_solution(7768178357983194786)
XLA Ops:
  0.0 0.0 copy-start
  0.0 2.2 %copy-done = bf16[128,16384]{1,0:T(8,128)(2,1)S(1)} copy-done((bf16[128,16384]{1,0:T(8,128)(2,1)S(1)}, bf16[128,16384]{1,0:T(8,128)(2,1)}, u32[]{:S(2)}) %copy-start) | copy-done | bytes 4194328
  2.2 0.0 copy-start.1
  2.2 1.2 %copy-done.1 = bf16[4096,128]{1,0:T(8,128)(2,1)S(1)} copy-done((bf16[4096,128]{1,0:T(8,128)(2,1)S(1)}, bf16[4096,128]{1,0:T(8,128)(2,1)}, u32[]{:S(2)}) %copy-start.1) | copy-done | bytes 1048600
  3.4 0.0 copy-start.2
  3.4 1.2 %copy-done.2 = bf16[4096,128]{1,0:T(8,128)(2,1)S(1)} copy-done((bf16[4096,128]{1,0:T(8,128)(2,1)S(1)}, bf16[4096,128]{1,0:T(8,128)(2,1)}, u32[]{:S(2)}) %copy-start.2) | copy-done | bytes 1048600
  4.6 0.0 copy-start.3
  4.6 1.2 %copy-done.3 = bf16[128,4096]{1,0:T(8,128)(2,1)S(1)} copy-done((bf16[128,4096]{1,0:T(8,128)(2,1)S(1)}, bf16[128,4096]{1,0:T(8,128)(2,1)}, u32[]{:S(2)}) %copy-start.3) | copy-done | bytes 1048600
  5.9 0.0 copy-start.4
  5.9 0.7 copy-done.4
  6.5 0.0 copy-start.5
  6.5 0.7 copy-done.5
  7.2 0.0 copy-start.6
  7.2 0.7 copy-done.6
  7.8 95.0 %shard_map.73 = bf16[128,4096]{1,0:T(8,128)(2,1)S(1)} custom-call(bf16[128,16384]{1,0:T(8,128)(2,1)S(1)} %copy-done, bf16[4096,128]{1,0:T(8,128)(2,1)S(1)} %copy-done.1, bf16[4096,128]{1,0:T(8,128)(2,1)S(1)} %copy-done.2, bf16[128,4096]{1,0:T(8,128)(2,1)S(1)} %copy-done.3, s32[128]{0:T(128)S(1)} %bitcast.3, s32[128]{0:T(128)S(1)} %bitcast.4, s32[128]{0:T(128)S(1)} %bitcast.5), custom_call_target="tpu_custom_call" | custom-call | flops 1610612736 | bytes 16777216 | tf_op jit(solution)/shard_map/pallas_call | solution.py:283
  102.8 1.0 copy.9
Async XLA Ops:
  0.0 2.2 %copy-start = (bf16[128,16384]{1,0:T(8,128)(2,1)S(1)}, bf16[128,16384]{1,0:T(8,128)(2,1)}, u32[]{:S(2)}) copy-start(bf16[128,16384]{1,0:T(8,128)(2,1)} %tok_hbm.1) | copy-start | bytes 12582916
  2.2 1.2 %copy-start.1 = (bf16[4096,128]{1,0:T(8,128)(2,1)S(1)}, bf16[4096,128]{1,0:T(8,128)(2,1)}, u32[]{:S(2)}) copy-start(bf16[4096,128]{1,0:T(8,128)(2,1)} %gate_hbm.1) | copy-start | bytes 3145732
  3.4 1.2 %copy-start.2 = (bf16[4096,128]{1,0:T(8,128)(2,1)S(1)}, bf16[4096,128]{1,0:T(8,128)(2,1)}, u32[]{:S(2)}) copy-start(bf16[4096,128]{1,0:T(8,128)(2,1)} %up_hbm.1) | copy-start | bytes 3145732
  4.6 1.2 %copy-start.3 = (bf16[128,4096]{1,0:T(8,128)(2,1)S(1)}, bf16[128,4096]{1,0:T(8,128)(2,1)}, u32[]{:S(2)}) copy-start(bf16[128,4096]{1,0:T(8,128)(2,1)} %down_hbm.1) | copy-start | bytes 3145732
  5.9 0.7 copy-start.4
  6.5 0.7 copy-start.5
  7.2 0.7 copy-start.6

commit v3 on v2

--- a/solution.py
+++ b/solution.py
@@ -9,7 +9,7 @@
 
 BS = 128
 MESH = pl.DeviceIdType.MESH
-CHUNKS = 4
+CHUNKS = 2
 
 
 def expand_mask(mask):
@@ -49,8 +49,8 @@
 
 
 def kernel(n, tok_hbm, gate_hbm, up_hbm, down_hbm, gmask_hbm, umask_hbm, dmask_hbm, out,
-           gmask, umask, dmask, T, W, PC, G, psend, precv, H,
-           ch_s, ch_r, ip_s, ip_r, y_s, y_r, tz_s, tz_r, tx_s, tx_r, tc_s, tc_r,
+           gmask, umask, dmask, T, W, D, PC, G, psend, precv, H,
+           ch_s, ch_r, ip_s, g_r, y_s, tz_s, tz_r, tx_s, tx_r, tc_s, tc_r,
            p_s, p_r, h_s, h_r, ld):
     g = lax.axis_index("groups")
     z = lax.axis_index("dp")
@@ -75,8 +75,7 @@
             device_id_type=MESH)
 
     own_cols = pl.ds(pl.multiple_of(z * width, 128), width)
-    load_down = pltpu.make_async_copy(
-        down_hbm.at[pl.ds(pl.multiple_of(g * half, half), half), :], PC.at[z], ld.at[0])
+    load_down = pltpu.make_async_copy(down_hbm, D, ld.at[0])
     load_tok = pltpu.make_async_copy(
         tok_hbm.at[:, own_cols], T.at[pl.ds(pl.multiple_of(z * rows, rows), rows), :], ld.at[1])
     load_gate = pltpu.make_async_copy(gate_hbm, W.at[:, pl.ds(0, hid)], ld.at[2])
@@ -85,27 +84,18 @@
         pltpu.make_async_copy(src, dst, ld.at[4 + m])
         for m, (src, dst) in enumerate(
             ((dmask_hbm, dmask), (gmask_hbm, gmask), (umask_hbm, umask)))]
-    load_masks[0].start()
-    load_down.start()
+    loads = [load_masks[0], load_down, load_masks[1], load_masks[2], load_gate, load_up, load_tok]
+    for load in loads:
+        load.start()
 
     barrier = pltpu.get_barrier_semaphore()
     for d in range(1, n):
         pl.semaphore_signal(barrier, inc=1, device_id={"dp": mod(z + d)}, device_id_type=MESH)
         pl.semaphore_signal(barrier, inc=1, device_id={"tensor": mod(t + d)}, device_id_type=MESH)
+        pl.semaphore_signal(
+            barrier, inc=1, device_id={"groups": 1 - g, "tensor": mod(t + d)}, device_id_type=MESH)
     pl.semaphore_signal(barrier, inc=1, device_id={"groups": 1 - g}, device_id_type=MESH)
-    load_masks[1].start()
-    load_masks[2].start()
-    load_gate.start()
-    load_up.start()
-    load_tok.start()
-
-    load_masks[0].wait()
-    load_down.wait()
-    for b in range(blocks):
-        keep = dmask[z * blocks + b].astype(jnp.float32)
-        cols = pl.ds(b * BS, BS)
-        PC[z, :, cols] = (PC[z, :, cols].astype(jnp.float32) * keep).astype(jnp.bfloat16)
-    pl.semaphore_wait(barrier, 2 * (n - 1) + 1)
+    pl.semaphore_wait(barrier, 3 * (n - 1) + 1)
 
     pending = []
 
@@ -119,52 +109,58 @@
     def chunk(c):
         return pl.ds(c * cw, cw)
 
+    def half_rows(h):
+        return pl.ds(pl.multiple_of(h * half, half), half)
+
     def g_rows(ts, h):
         return pl.ds(pl.multiple_of(ts * hid + h * half, half), half)
+
+    far = jnp.where(2 * z < n, n - 1, 0)
+
+    def side(a):
+        return lax.div(a, 2)
+
+    def relayed(src, k):
+        return (side(src) != side(k)) & (k != z) & (k != far)
 
     def chain(direction, r, c):
         k = z - r if direction == 0 else z + r
         to = z + 1 if direction == 0 else z - 1
         ok = (k >= 0) & (to < n) if direction == 0 else (k < n) & (to >= 0)
         kk = mod(k)
+        src = D.at[half_rows(g), chunk(c)] if r == 0 else PC.at[kk, :, chunk(c)]
         return remote(
-            PC.at[kk, :, chunk(c)], PC.at[kk, :, chunk(c)], ch_s.at[direction, r, c],
+            src, PC.at[kk, :, chunk(c)], ch_s.at[direction, r, c],
             ch_r.at[direction, r, c], dp=mod(to)), ok
 
     def dispatch(k, slot, c, ok):
-        copy = remote(
-            PC.at[k, :, chunk(c)], G.at[g_rows(t, g), chunk(c)], ip_s.at[slot, c],
-            ip_r.at[t, c], tensor=k)
-        go(copy, ok & (k != t))
+        src = PC.at[k, :, chunk(c)]
+        dst = G.at[g_rows(t, g), chunk(c)]
+        go(remote(src, dst, ip_s.at[slot, 0, c], g_r.at[t, g, c], tensor=k), ok & (k != t))
+        go(remote(src, dst, ip_s.at[slot, 1, c], g_r.at[t, g, c], groups=1 - g, tensor=k),
+           ok & jnp.logical_not(relayed(t, k)))
+
+        @pl.when(ok & (k == t))
+        def _():
+            G[g_rows(t, g), chunk(c)] = PC[t, :, chunk(c)]
+
+    def arrival(ts, h, c):
+        ref = G.at[g_rows(ts, h), chunk(c)]
+        return remote(ref, ref, y_s.at[0, 0], g_r.at[ts, h, c], groups=1 - g)
 
     def across(e, c):
-        ts = mod(t + e)
+        ts = mod((1 - side(t)) * 2 + e)
         ref = G.at[g_rows(ts, g), chunk(c)]
-        return remote(ref, ref, y_s.at[e, c], y_r.at[e, c], groups=1 - g)
-
-    def arrived(e, c):
-        ts = mod(t + e)
-        ref = G.at[g_rows(ts, g), chunk(c)]
-        return remote(ref, ref, ip_s.at[0, c], ip_r.at[ts, c], tensor=ts)
-
-    crossings = [[across(e, c) for e in range(n)] for c in range(CHUNKS)]
-
-    def owner_round(r):
-        @pl.when(jnp.abs(z - t) == r)
+        return remote(ref, ref, y_s.at[e, c], g_r.at[ts, g, c], groups=1 - g)
+
+    crossings = [[across(e, c) for e in range(2)] for c in range(CHUNKS)]
+
+    def owner_round(r, c):
+        @pl.when((jnp.abs(z - t) == r) & (t != far))
         def _():
-            for c in range(CHUNKS):
-                G[g_rows(t, g), chunk(c)] = PC[t, :, chunk(c)]
-                crossings[c][0].start()
-                for e in range(1, n):
-                    arrived(e, c).wait_recv()
-                    crossings[c][e].start()
-
-    for c in range(CHUNKS):
-        for direction in range(2):
-            copy, ok = chain(direction, 0, c)
-            go(copy, ok)
-    for c in range(CHUNKS):
-        dispatch(z, 0, c, True)
+            for e in range(2):
+                arrival(mod((1 - side(t)) * 2 + e), g, c).wait_recv()
+                crossings[c][e].start()
 
     def token_piece(s, q):
         return T.at[pl.ds(pl.multiple_of(s * rows + q * quarter, quarter), quarter), :]
@@ -175,6 +171,27 @@
             tok_hbm.at[pl.ds(pl.multiple_of(t * quarter, quarter), quarter),
                        pl.ds(pl.multiple_of(k * width, 128), width)],
             token_piece(z, t), tz_s.at[d - 1], tz_r.at[d - 1], dp=k))
+
+    load_masks[0].wait()
+    load_down.wait()
+    for b in range(blocks):
+        keep = dmask[z * blocks + b].astype(jnp.float32)
+        cols = pl.ds(b * BS, BS)
+        D[:, cols] = (D[:, cols].astype(jnp.float32) * keep).astype(jnp.bfloat16)
+
+    for c in range(CHUNKS):
+        for direction in range(2):
+            copy, ok = chain(direction, 0, c)
+            go(copy, ok)
+    for c in range(CHUNKS):
+        for h in range(2):
+            rows_h = pl.ds(h * half, half)
+            go(remote(D.at[rows_h, chunk(c)], G.at[g_rows(t, h), chunk(c)],
+                      ip_s.at[0, h, c], g_r.at[t, h, c], tensor=z), z != t)
+
+    @pl.when(z == t)
+    def _():
+        G[pl.ds(pl.multiple_of(t * hid, hid), hid), :] = D[...]
 
     def relay_tokens(d):
         s = mod(z - d)
@@ -218,28 +235,41 @@
 
     load_tok.wait()
     own = products(z)
-    owner_round(0)
-
-    for r in range(1, n):
+
+    def chain_step(r, c):
+        for direction in range(2):
+            k = z - r if direction == 0 else z + r
+            ok = k >= 0 if direction == 0 else k < n
+            kk = mod(k)
+            piece = PC.at[kk, :, chunk(c)]
+            came = remote(piece, piece, ch_s.at[direction, r - 1, c],
+                          ch_r.at[direction, r - 1, c], dp=mod(z + 1))
+            pl.when(ok)(came.wait_recv)
+            if r < n - 1:
+                copy, also = chain(direction, r, c)
+                go(copy, ok & also)
+            dispatch(kk, 2 * r - 1 + direction, c, ok)
+        if r < n - 1 and c > 0:
+            owner_round(r, c - 1)
+
+    def chain_round(r):
         for c in range(CHUNKS):
-            for direction in range(2):
-                k = z - r if direction == 0 else z + r
-                ok = k >= 0 if direction == 0 else k < n
-                kk = mod(k)
-                piece = PC.at[kk, :, chunk(c)]
-                came = remote(piece, piece, ch_s.at[direction, r - 1, c],
-                              ch_r.at[direction, r - 1, c], dp=mod(z + 1))
-                pl.when(ok)(came.wait_recv)
-                if r < n - 1:
-                    copy, also = chain(direction, r, c)
-                    go(copy, ok & also)
-                dispatch(kk, 2 * r - 1 + direction, c, ok)
-        owner_round(r)
-        relay_tokens((1, 3, 2)[r - 1])
-    for d in (1, 3, 2):
-        relay_x(d)
-    for d in (1, 3, 2):
-        finish_tokens(d)
+            chain_step(r, c)
+
+    relay_tokens(1)
+    relay_tokens(3)
+    chain_round(1)
+    relay_tokens(2)
+    relay_x(1)
+    relay_x(3)
+    owner_round(1, CHUNKS - 1)
+    chain_round(2)
+    relay_x(2)
+    owner_round(2, CHUNKS - 1)
+    finish_tokens(1)
+    finish_tokens(3)
+    finish_tokens(2)
+    chain_round(3)
 
     total = own
     for d in range(1, n):
@@ -256,10 +286,11 @@
         remote(theirs, theirs, h_s.at[d - 1], h_r.at[d - 1], tensor=mod(t + d)).wait_recv()
 
     for c in range(CHUNKS):
-        for e in range(n):
-            ts = mod(t + e)
-            ref = G.at[g_rows(ts, 1 - g), chunk(c)]
-            remote(ref, ref, y_s.at[e, c], y_r.at[e, c], groups=1 - g).wait_recv()
+        for ts in range(n):
+            for h in range(2):
+                held = (t == ts) & ((z == t) | (g == h))
+                passed = (g == h) & relayed(ts, t)
+                pl.when(jnp.logical_not(held | passed))(arrival(jnp.int32(ts), jnp.int32(h), c).wait_recv)
         out[:, chunk(c)] = jnp.dot(
             H[...], G[:, chunk(c)], preferred_element_type=jnp.float32).astype(jnp.bfloat16)
 
@@ -268,9 +299,12 @@
             copy.wait_send()
         else:
             pl.when(cond)(copy.wait_send)
-    for row in crossings:
-        for copy in row:
-            copy.wait_send()
+
+    @pl.when((z != t) & (t != far))
+    def _():
+        for row in crossings:
+            for copy in row:
+                copy.wait_send()
 
 
 def fused(n, tokens, gate_weight, up_weight, down_weight, gate_mask, up_mask, down_mask):
@@ -289,14 +323,15 @@
             flags, flags, flags,
             pltpu.VMEM((n * rows, width), bf16),
             pltpu.VMEM((width, 2 * hid), bf16),
+            pltpu.VMEM((hid, width), bf16),
             pltpu.VMEM((n, hid // 2, width), bf16),
             pltpu.VMEM((n * hid, width), bf16),
             pltpu.VMEM((n - 1, rows, 2 * hid), bf16),
             pltpu.VMEM((n - 1, rows, 2 * hid), bf16),
             pltpu.VMEM((rows, n * hid), bf16),
             dma((2, n - 1, CHUNKS)), dma((2, n - 1, CHUNKS)),
-            dma((2 * n - 1, CHUNKS)), dma((n, CHUNKS)),
-            dma((n, CHUNKS)), dma((n, CHUNKS)),
+            dma((2 * n - 1, 2, CHUNKS)), dma((n, 2, CHUNKS)),
+            dma((2, CHUNKS)),
             dma((n - 1,)), dma((n - 1,)),
             dma((n - 1,)), dma((n - 1,)),
             dma((2, n - 1)), dma((2, n - 1)),
@@ -305,7 +340,7 @@
             dma((7,)),
         ],
         compiler_params=pltpu.CompilerParams(
-            collective_id=0, has_side_effects=True, vmem_limit_bytes=40 * 1024 * 1024),
+            collective_id=0, has_side_effects=True, vmem_limit_bytes=63 * 1024 * 1024),
         cost_estimate=pl.CostEstimate(
             flops=2 * rows * n * width * 3 * hid, bytes_accessed=16 * 1024 * 1024,
             transcendentals=rows * hid),

time: 104 us -> 95.6 us (0.919)
  local copies, waits for them, and re-layouts: 8.8 us -> 2.29 us
  Pallas kernels: 95 us -> 92.5 us
    unnamed x15 -> x1, local copies, waits for them, and re-layouts: 8.8 us -> 2.29 us
    pallas_call x1, Pallas kernels: 95 us -> 92.5 us  [fused(): pl.pallas_call(functools.partial(kernel, n), out_shape=jax.ShapeDtypeStru...]
where the time goes in v3:
time: 95.6 us; the launch traced here: 94.7 us
  Pallas kernels  92.5 us (97%)
  local copies, waits for them, and re-layouts  2.29 us (2%)
    pallas_call x1, Pallas kernels, fused(): pl.pallas_call(functools.partial(kernel, n), out_shape=jax.ShapeDtypeStru...  92.5 us
    unnamed x1, local copies, waits for them, and re-layouts  2.29 us

profile of v3, /device:TPU:3, one launch (start us, length us, event | category | flops | bytes accessed | tf_op | source)
XLA Modules:
  0.0 94.7 jit_solution(3306937343142984477)
XLA Ops:
  0.0 92.5 %shard_map.73 = bf16[128,4096]{1,0:T(8,128)(2,1)} custom-call(bf16[128,16384]{1,0:T(8,128)(2,1)} %tok_hbm.1, bf16[4096,128]{1,0:T(8,128)(2,1)} %gate_hbm.1, bf16[4096,128]{1,0:T(8,128)(2,1)} %up_hbm.1, bf16[128,4096]{1,0:T(8,128)(2,1)} %down_hbm.1, s32[128]{0:T(128)} %bitcast.3, s32[128]{0:T(128)} %bitcast.4, s32[128]{0:T(128)} %bitcast.5), custom_call_target="tpu_custom_call" | custom-call | flops 1610612736 | bytes 16777216 | tf_op jit(solution)/shard_map/pallas_call | solution.py:317
  92.5 2.3 %copy.9 = bf16[128,4096]{1,0:T(8,128)(2,1)} copy(bf16[128,4096]{1,0:T(8,128)(2,1)} %shard_map.73) | data formatting | bytes 2097152

commit v4 on v3

--- a/solution.py
+++ b/solution.py
@@ -183,12 +183,6 @@
         for direction in range(2):
             copy, ok = chain(direction, 0, c)
             go(copy, ok)
-    for c in range(CHUNKS):
-        for h in range(2):
-            rows_h = pl.ds(h * half, half)
-            go(remote(D.at[rows_h, chunk(c)], G.at[g_rows(t, h), chunk(c)],
-                      ip_s.at[0, h, c], g_r.at[t, h, c], tensor=z), z != t)
-
     @pl.when(z == t)
     def _():
         G[pl.ds(pl.multiple_of(t * hid, hid), hid), :] = D[...]
@@ -266,6 +260,12 @@
     chain_round(2)
     relay_x(2)
     owner_round(2, CHUNKS - 1)
+    for c in range(CHUNKS):
+        for h in range(2):
+            rows_h = pl.ds(h * half, half)
+            go(remote(D.at[rows_h, chunk(c)], G.at[g_rows(t, h), chunk(c)],
+                      ip_s.at[0, h, c], g_r.at[t, h, c], tensor=z), z != t)
+
     finish_tokens(1)
     finish_tokens(3)
     finish_tokens(2)

time: 95.6 us -> 89.9 us (0.940)
  Pallas kernels: 92.5 us -> 87.4 us
    pallas_call x1, Pallas kernels: 92.5 us -> 87.4 us  [fused(): pl.pallas_call(functools.partial(kernel, n), out_shape=jax.ShapeDtypeStru...]
where the time goes in v4:
time: 89.9 us; the launch traced here: 89.7 us
  Pallas kernels  87.4 us (97%)
  local copies, waits for them, and re-layouts  2.29 us (3%)
    pallas_call x1, Pallas kernels, fused(): pl.pallas_call(functools.partial(kernel, n), out_shape=jax.ShapeDtypeStru...  87.4 us
    unnamed x1, local copies, waits for them, and re-layouts  2.29 us

profile of v4, /device:TPU:3, one launch (start us, length us, event | category | flops | bytes accessed | tf_op | source)
XLA Modules:
  0.0 89.7 jit_solution(12591923597916518025)
XLA Ops:
  0.0 87.4 %shard_map.73 = bf16[128,4096]{1,0:T(8,128)(2,1)} custom-call(bf16[128,16384]{1,0:T(8,128)(2,1)} %tok_hbm.1, bf16[4096,128]{1,0:T(8,128)(2,1)} %gate_hbm.1, bf16[4096,128]{1,0:T(8,128)(2,1)} %up_hbm.1, bf16[128,4096]{1,0:T(8,128)(2,1)} %down_hbm.1, s32[128]{0:T(128)} %bitcast.3, s32[128]{0:T(128)} %bitcast.4, s32[128]{0:T(128)} %bitcast.5), custom_call_target="tpu_custom_call" | custom-call | flops 1610612736 | bytes 16777216 | tf_op jit(solution)/shard_map/pallas_call | solution.py:317
  87.4 2.3 %copy.9 = bf16[128,4096]{1,0:T(8,128)(2,1)} copy(bf16[128,4096]{1,0:T(8,128)(2,1)} %shard_map.73) | data formatting | bytes 2097152
